TPU v7x, 32 devices: a whole 2x2x4 slice. The times are simulated.
32 devices in a mesh: row: 8 (over y, x, core), col: 4 (over z).
Axes of the slice: x: 2, y: 2, z: 4, core: 2. Of those that a mesh axis runs over, the one named last changes fastest.
Arguments:
- amp_tiles: float32 [8, 4, 256, 256], P('row', 'col'), may hold values from -6 to 6
- pool_tiles: float32 [4, 256, 16, 256], P('col', 'row'), may hold values from -0.0546875 to 0.0546875
- task_amp: int32 [8, 4, 48], P('row', 'col'), may hold values from 0 to 3
- task_pool: int32 [8, 4, 48], P('row', 'col'), may hold values from 0 to 15
- task_out: int32 [8, 4, 48], P('row', 'col'), may hold values from 0 to 7
- task_live: int32 [8, 4, 48], P('row', 'col'), may hold values from 0 to 1, as said below
Outputs:
- result_tiles: float32 [4, 256, 8, 256], P('col', 'row')
Inputs may be any that keep to these rules, and one draw needn't show every extreme that they name: `task_live`: on every device the live tasks come first; each device has at least a quarter of 48 live tasks, and some device has all 48 live.
All inputs are finite; a program needn't handle non-finite values.
Results may differ from a plain program's by a relative error of at most 0.0003.
Values sent between devices are 32-bit elements; how exact they have to be, the bound alone decides.
A program may use at most 128 MiB of HBM per device.

v0:
```python
import jax
import jax.numpy as jnp
from jax import lax
from jax.sharding import PartitionSpec as P

OUT_POOL = 8


def add_terms(piece, chosen, pool_index, weights):
    integral = jnp.take(piece[0], pool_index, axis=1)
    product = jnp.einsum("tik,ktj->tij", chosen, integral, precision=lax.Precision.HIGHEST)
    return jnp.einsum("to,tij->ioj", weights, product, precision=lax.Precision.HIGHEST)


def per_device(amp_tiles, pool_tiles, task_amp, task_pool, task_out, task_live):
    slots = jnp.arange(OUT_POOL, dtype=jnp.int32)
    gathered = lax.all_gather(amp_tiles, "col", axis=1, tiled=True)
    chosen = jnp.take(gathered[0], task_amp[0, 0], axis=0)
    pool_index = task_pool[0, 0]
    live = task_live[0, 0].astype(jnp.float32)
    weights = (task_out[0, 0][:, None] == slots[None, :]).astype(jnp.float32) * live[:, None]
    whole_pool = lax.all_gather(pool_tiles, "row", axis=1, tiled=True)
    partial_value = add_terms(whole_pool, chosen, pool_index, weights)
    owned = lax.psum_scatter(partial_value, "row", scatter_dimension=0, tiled=True)
    return owned[None]


def solution(mesh):
    in_specs = (
        P("row", "col", None, None),
        P("col", "row", None, None),
        P("row", "col", None),
        P("row", "col", None),
        P("row", "col", None),
        P("row", "col", None),
    )
    out_specs = P("col", "row", None, None)
    return jax.shard_map(
        per_device, mesh=mesh, in_specs=in_specs, out_specs=out_specs, check_vma=False
    )
```

profile of v0, /device:TPU:0, one launch (start us, length us, event | category | flops | bytes accessed | tf_op | source)
XLA Modules:
  0.0 172.9 jit_solution(6740030071859971109)
XLA Ops:
  6.5 0.0 all-gather.3.cloned.1.call-start
  6.5 0.7 all-gather.3.cloned.1.call-update
  7.3 0.0 all-gather.5.cloned.1.call-start
  7.3 2.1 %copy.9 = f32[1,32,16,256]{3,1,2,0:T(8,128)} copy(f32[1,32,16,256]{3,2,1,0:T(8,128)} %param.7) | data formatting | bytes 1048576 | tf_op args[1]
  9.5 0.0 all-gather.5.cloned.1.call-update
  9.5 0.0 reduce-scatter.2.cloned.1.call-start
  9.5 0.7 fusion.18
  10.2 0.7 fusion.17
  10.9 0.7 convert_bitcast_fusion
  11.5 0.7 compare_and_fusion
  12.2 27.4 %all-gather.3.cloned.1.call-done = f32[1,4,256,256]{3,2,0,1:T(8,128)} async-done(((f32[1,1,256,256]{3,2,0,1:T(8,128)}), f32[1,4,256,256]{3,2,0,1:T(8,128)}) %all-gather.3.cloned.1.call-update) | async-done | bytes 1048592 | tf_op jit(solution)/shard_map/all_gather | solution.py:17
  39.6 8.9 %gather_fusion = f32[48,256,256]{2,1,0:T(8,128)} fusion(f32[4,256,256]{2,1,0:T(8,128)} %bitcast.27, s32[1024]{0:T(1024)S(1)} %pad_clamp_fusion.1), kind=kCustom, calls=%fused_computation | custom fusion | bytes 25166016 | tf_op jit(solution)/shard_map/jit(_take)/gather | solution.py:18
  48.5 29.3 %all-gather.5.cloned.1.call-done = f32[1,256,16,256]{3,1,2,0:T(8,128)} async-done(((f32[1,32,16,256]{3,1,2,0:T(8,128)}), f32[1,256,16,256]{3,1,2,0:T(8,128)}) %all-gather.5.cloned.1.call-update) | async-done | bytes 4194320 | tf_op jit(solution)/shard_map/all_gather | solution.py:22
  77.7 9.8 %gather_fusion.1 = f32[48,256,256]{2,1,0:T(8,128)} fusion(f32[256,16,256]{2,0,1:T(8,128)} %bitcast.28, s32[1024]{0:T(1024)S(1)} %pad_clamp_fusion), kind=kCustom, calls=%fused_computation.1 | custom fusion | bytes 25166016 | tf_op jit(solution)/shard_map/jit(_take)/gather | solution.py:10
  87.5 0.0 copy-start
  87.5 18.9 %fusion = f32[48,256,256]{2,1,0:T(8,128)} fusion(f32[48,256,256]{2,1,0:T(8,128)} %gather_fusion.1, f32[48,256,256]{2,1,0:T(8,128)} %gather_fusion, pred[48]{0:T(512)(128)(4,1)S(1)} %get-tuple-element.5, pred[48]{0:T(512)(128)(4,1)S(1)} %get-tuple-element.6), kind=kOutput, calls=%fused_computation.2 | convolution fusion | flops 9669967872 | bytes 37748832 | tf_op jit(solution)/shard_map/tik,ktj->tij/dot_general | solution.py:11
  106.4 0.0 copy-done
  106.4 18.6 %fusion.9 = f32[256,8,256]{2,1,0:T(8,128)} fusion(f32[48,256,256]{2,1,0:T(8,128)} %fusion, f32[48]{0:T(128)S(1)} %convert_bitcast_fusion, s32[48]{0:T(128)S(1)} %bitcast.30), kind=kOutput, calls=%fused_computation.11 | convolution fusion | flops 301990656 | bytes 14680448 | tf_op jit(solution)/shard_map/to,tij->ioj/dot_general | solution.py:12
  125.0 0.0 reduce-scatter.2.cloned.1.call-update
  125.0 41.4 %reduce-scatter.2.cloned.1.call-done = f32[32,8,256]{2,1,0:T(8,128)} async-done(((f32[256,8,256]{2,1,0:T(8,128)}), f32[32,8,256]{2,1,0:T(8,128)}) %reduce-scatter.2.cloned.1.call-update) | async-done | bytes 262160 | tf_op jit(solution)/shard_map/reduce_scatter | solution.py:24
  (2 shorter events, 0.0 us)
Async XLA Ops:
  6.5 33.1 %all-gather.3.cloned.1.call-start = ((), (), s32[]{:S(2)}) async-start(), calls=%async_computation.1 | async-start | bytes 1310720 | tf_op jit(solution)/shard_map/all_gather | solution.py:17
  7.3 70.5 %all-gather.5.cloned.1.call-start = ((), (), s32[]{:S(2)}) async-start(), calls=%async_computation.2 | async-start | bytes 4718592 | tf_op jit(solution)/shard_map/all_gather | solution.py:22
  9.5 156.9 %reduce-scatter.2.cloned.1.call-start = ((), (), s32[]{:S(2)}) async-start(), calls=%async_computation.3 | async-start | bytes 2359296 | tf_op jit(solution)/shard_map/reduce_scatter | solution.py:24
  87.5 18.9 %copy-start = (s32[1,1,48]{2,1,0:T(1,128)S(1)}, s32[1,1,48]{2,1,0:T(1,128)}, u32[]{:S(2)}) copy-start(s32[1,1,48]{2,1,0:T(1,128)} %param.10) | copy-start | bytes 580
Sparse Core Ops, SparseCore 0:
  8.9 30.6 all-gather.2
  41.5 36.1 all-gather.4
  125.1 41.1 reduce-scatter.1
where the time goes:
time: 173 us
  waiting for transfers between devices  98.8 us (57%)
  matrix products  37.5 us (22%)
  local copies, waits for them, and re-layouts  20.8 us (12%)
  between operations  13.1 us (8%)
  other arithmetic  2.67 us (2%)
    reduce_scatter x1, waiting for transfers between devices, per_device(): lax.psum_scatter(partial_value, 'row', scatter_dimension=0, tiled=True)  41.4 us
    all_gather x1, waiting for transfers between devices, per_device(): whole_pool = lax.all_gather(pool_tiles, 'row', axis=1, tiled=True)  29.3 us
    all_gather x1, waiting for transfers between devices, per_device(): gathered = lax.all_gather(amp_tiles, 'col', axis=1, tiled=True)  27.4 us
    dot_general x1, matrix products, add_terms(): jnp.einsum('tik,ktj->tij', chosen, integral, precision=lax.Precision.HIGH...  18.9 us
    dot_general x1, matrix products, add_terms(): jnp.einsum('to,tij->ioj', weights, product, precision=lax.Precision.HIGHEST)  18.6 us
    gather x1, local copies, waits for them, and re-layouts, add_terms(): integral = jnp.take(piece[0], pool_index, axis=1)  9.75 us
    gather x1, local copies, waits for them, and re-layouts, per_device(): chosen = jnp.take(gathered[0], task_amp[0, 0], axis=0)  8.86 us
  transfers between devices with their start and end apart: 3, of which 3 were waited for; matrix products, arithmetic and copies ran while one was open for 8% of the time, Pallas kernels for 0%

commit v1 on v0

--- a/solution.py
+++ b/solution.py
@@ -1,9 +1,14 @@
+import functools
+
 import jax
 import jax.numpy as jnp
 from jax import lax
+from jax.experimental import pallas as pl
+from jax.experimental.pallas import tpu as pltpu
 from jax.sharding import PartitionSpec as P
 
 OUT_POOL = 8
+MESH = pl.DeviceIdType.MESH
 
 
 def add_terms(piece, chosen, pool_index, weights):
@@ -12,7 +17,7 @@
     return jnp.einsum("to,tij->ioj", weights, product, precision=lax.Precision.HIGHEST)
 
 
-def per_device(amp_tiles, pool_tiles, task_amp, task_pool, task_out, task_live):
+def gathered_plan(amp_tiles, pool_tiles, task_amp, task_pool, task_out, task_live):
     slots = jnp.arange(OUT_POOL, dtype=jnp.int32)
     gathered = lax.all_gather(amp_tiles, "col", axis=1, tiled=True)
     chosen = jnp.take(gathered[0], task_amp[0, 0], axis=0)
@@ -25,7 +30,290 @@
     return owned[None]
 
 
+def halves(value):
+    high = value.astype(jnp.bfloat16)
+    low = (value - high.astype(jnp.float32)).astype(jnp.bfloat16)
+    return high, low
+
+
+def kernel(
+    n_row, n_col, slab, pool,
+    amp_ref, pool_ref, t_amp, t_pool, t_out, t_live, out_ref,
+    v_all, v_hi, v_lo, a_all, m_hi, m_lo, info,
+    v_send, v_recv, p_send, p_recv, i_send, i_recv, z_send, z_recv, own_sem,
+):
+    r = lax.axis_index("row")
+    c = lax.axis_index("col")
+    sib = r + 1 - 2 * (r % 2)
+    x_of = r + 2 - 4 * ((r // 2) % 2)
+    y_of = r + 4 - 8 * (r // 4)
+    d_of = x_of + 4 - 8 * (r // 4)
+    vrows = slab * pool * 2
+    half = vrows // 2
+    tasks = t_amp.shape[1]
+    arows = slab * 2
+    blk = n_row * arows
+    chunk = blk // 2
+
+    barrier = pltpu.get_barrier_semaphore()
+    for d in range(1, n_row):
+        pl.semaphore_signal(barrier, inc=1, device_id=(lax.rem(r + d, n_row), c), device_id_type=MESH)
+
+    @pl.when(c > 0)
+    def _():
+        pl.semaphore_signal(barrier, inc=1, device_id=(r, c - 1), device_id_type=MESH)
+
+    @pl.when(c < n_col - 1)
+    def _():
+        pl.semaphore_signal(barrier, inc=1, device_id=(r, c + 1), device_id_type=MESH)
+
+    info[r] = jnp.full((8, 128), -1.0, jnp.float32)
+    info[r, 0:1, 0:tasks] = t_amp[...].astype(jnp.float32)
+    place = (t_pool[...] * OUT_POOL + t_out[...]).astype(jnp.float32)
+    info[r, 1:2, 0:tasks] = jnp.where(t_live[...] > 0, place, -1.0)
+
+    a_row = pl.multiple_of(c * blk + r * arows, 8)
+    own_a = pltpu.make_async_copy(
+        amp_ref.at[pl.ds(pl.multiple_of(r * arows, 8), arows)], a_all.at[pl.ds(a_row, arows)], own_sem.at[0])
+    own_a.start()
+    own_v = pltpu.make_async_copy(
+        pool_ref, v_all.at[pl.ds(pl.multiple_of(r * vrows, 8), vrows)], own_sem.at[1])
+    own_v.start()
+
+    near = (c + n_col - 1) // n_col + (2 * n_col - 2 - c) // n_col
+    pl.semaphore_wait(barrier, n_row - 1 + near)
+
+    plane = []
+    for d in (6, 2, 4, 3, 5, 7, 1):
+        to = lax.rem(r + d, n_row)
+        copy = pltpu.make_async_remote_copy(
+            src_ref=amp_ref.at[pl.ds(pl.multiple_of(to * arows, 8), arows)],
+            dst_ref=a_all.at[pl.ds(a_row, arows)],
+            send_sem=p_send.at[d], recv_sem=p_recv.at[d],
+            device_id=(to, c), device_id_type=MESH)
+        copy.start()
+        plane.append(copy)
+
+    def v_copy(index, origin, part, to, own=False):
+        rows = pl.ds(pl.multiple_of(origin * vrows + part * half, 8), half)
+        src = pool_ref.at[pl.ds(part * half, half)] if own else v_all.at[rows]
+        return pltpu.make_async_remote_copy(
+            src_ref=src, dst_ref=v_all.at[rows],
+            send_sem=v_send.at[index], recv_sem=v_recv.at[index],
+            device_id=(to, c), device_id_type=MESH)
+
+    v = [
+        v_copy(0, r, 0, x_of, True), v_copy(1, r, 1, x_of, True),
+        v_copy(2, r, 1, y_of, True), v_copy(3, r, 0, y_of, True),
+        v_copy(4, r, 0, sib, True), v_copy(5, r, 1, sib, True),
+        v_copy(6, x_of, 0, y_of), v_copy(7, x_of, 0, sib),
+        v_copy(8, y_of, 1, x_of), v_copy(9, y_of, 1, sib),
+        v_copy(10, x_of, 1, sib), v_copy(11, y_of, 0, sib),
+        v_copy(12, d_of, 0, sib), v_copy(13, d_of, 1, sib),
+    ]
+    for index in (0, 2, 1, 3, 4, 5):
+        v[index].start()
+
+    lists = []
+    for d in range(1, n_row):
+        copy = pltpu.make_async_remote_copy(
+            src_ref=info.at[r], dst_ref=info.at[r],
+            send_sem=i_send.at[d], recv_sem=i_recv.at[d],
+            device_id=(lax.rem(r + d, n_row), c), device_id_type=MESH)
+        copy.start()
+        lists.append(copy)
+
+    def z_copy(way, step, part):
+        tile = c - step if way == 0 else c + step
+        to = c + 1 if way == 0 else c - 1
+        rows = pl.ds(pl.multiple_of(tile * blk + part * chunk, 8), chunk)
+        slot = ((way * (n_col - 1)) + step) * 2 + part
+        return pltpu.make_async_remote_copy(
+            src_ref=a_all.at[rows], dst_ref=a_all.at[rows],
+            send_sem=z_send.at[slot], recv_sem=z_recv.at[slot],
+            device_id=(r, to), device_id_type=MESH)
+
+    def z_sends(way, step):
+        if way == 0:
+            return jnp.logical_and(c - step >= 0, c < n_col - 1)
+        return jnp.logical_and(c + step < n_col, c > 0)
+
+    def z_gets(way, step):
+        return c - step - 1 >= 0 if way == 0 else c + step + 1 < n_col
+
+    def z_start(step, part):
+        for way in range(2):
+            @pl.when(z_sends(way, step))
+            def _():
+                z_copy(way, step, part).start()
+
+    def z_land(step, part):
+        for way in range(2):
+            @pl.when(z_gets(way, step))
+            def _():
+                z_copy(way, step, part).wait_recv()
+        if step + 1 < n_col - 1:
+            z_start(step + 1, part)
+
+    def split_pool(origin):
+        def one(p, carry):
+            first = origin * vrows + (p // 8) * 16 + p % 8
+            rows = [v_all[pl.ds(first + 8 * side, slab, stride=2 * pool), :] for side in range(2)]
+            high, low = halves(jnp.concatenate(rows, axis=1))
+            at = pl.ds(pl.multiple_of(origin * slab, 16), slab)
+            v_hi[p, at, :] = high
+            v_lo[p, at, :] = low
+            return carry
+        lax.fori_loop(0, pool, one, 0, unroll=4)
+
+    own_a.wait()
+    for copy in plane:
+        copy.wait_recv()
+    z_start(0, 0)
+    z_start(0, 1)
+    own_v.wait()
+    split_pool(r)
+    for copy in lists:
+        copy.wait_recv()
+    entry = lax.broadcasted_iota(jnp.int32, (pool * OUT_POOL, 128), 0).astype(jnp.float32)
+    line = lax.broadcasted_iota(jnp.int32, (2 * n_col * n_row, 128), 0)
+    line_row = line % n_row
+    line_amp = ((line // n_row) % n_col).astype(jnp.float32)
+    ends, starts = [], []
+    for other in range(n_row):
+        ends.append(jnp.where(entry == info[other, 1:2, :], 1.0, 0.0))
+        starts.append(jnp.where(jnp.logical_and(line_row == other, line_amp == info[other, 0:1, :]), 1.0, 0.0))
+    count = lax.dot_general(
+        jnp.concatenate(ends, axis=1).astype(jnp.bfloat16),
+        jnp.concatenate(starts, axis=1).astype(jnp.bfloat16),
+        (((1,), (1,)), ((), ())), preferred_element_type=jnp.float32).astype(jnp.bfloat16)
+
+    z_land(0, 0)
+    v[0].wait_recv()
+    v[6].start()
+    v[7].start()
+    v[2].wait_recv()
+    v[8].start()
+    v[9].start()
+    z_land(0, 1)
+    for index in (4, 5):
+        v[index].wait_recv()
+    split_pool(sib)
+    if n_col > 2:
+        z_land(1, 0)
+        z_land(1, 1)
+    v[1].wait_recv()
+    v[10].start()
+    v[3].wait_recv()
+    v[11].start()
+    split_pool(x_of)
+    split_pool(y_of)
+    for step in range(2, n_col - 1):
+        z_land(step, 0)
+    v[6].wait_recv()
+    v[12].start()
+    v[8].wait_recv()
+    v[13].start()
+    split_pool(d_of)
+    for step in range(2, n_col - 1):
+        z_land(step, 1)
+
+    def spread(pair, carry):
+        parts = []
+        for k in range(2):
+            i = pair * 2 + k
+            first = (i // 8) * 16 + i % 8
+            rows = [a_all[pl.ds(first + 8 * side, n_col * n_row, stride=arows), :] for side in range(2)]
+            high, low = halves(jnp.concatenate(rows, axis=1))
+            made = jnp.dot(count, jnp.concatenate([high, low], axis=0), preferred_element_type=jnp.float32)
+            parts.append(made.reshape(pool, OUT_POOL, made.shape[1]))
+        high, low = halves(jnp.concatenate(parts, axis=1))
+        at = pl.ds(pl.multiple_of(pair * 16, 16), 16)
+        m_hi[:, at, :] = high
+        m_lo[:, at, :] = low
+        return carry
+    lax.fori_loop(0, slab // 2, spread, 0, unroll=2)
+
+    for index in (7, 9, 10, 11, 12, 13):
+        v[index].wait_recv()
+    sib_x = x_of + 1 - 2 * (r % 2)
+    sib_y = y_of + 1 - 2 * (r % 2)
+    sib_d = d_of + 1 - 2 * (r % 2)
+    split_pool(sib_x)
+    split_pool(sib_y)
+    split_pool(sib_d)
+
+    total = jnp.zeros(out_ref.shape, jnp.float32)
+    for p in range(pool):
+        total = total + jnp.dot(m_hi[p], v_hi[p], preferred_element_type=jnp.float32)
+        total = total + jnp.dot(m_hi[p], v_lo[p], preferred_element_type=jnp.float32)
+        total = total + jnp.dot(m_lo[p], v_hi[p], preferred_element_type=jnp.float32)
+    out_ref[...] = total
+
+    for copy in plane + lists + v:
+        copy.wait_send()
+    for step in range(n_col - 1):
+        for way in range(2):
+            @pl.when(z_sends(way, step))
+            def _():
+                for part in range(2):
+                    z_copy(way, step, part).wait_send()
+
+
+def by_side(rows):
+    count, width = rows.shape
+    blocks = rows.reshape(count // 8, 8, 2, width // 2).transpose(0, 2, 1, 3)
+    return blocks.reshape(2 * count, width // 2)
+
+
+def slab_plan(n_row, n_col, amp_tiles, pool_tiles, task_amp, task_pool, task_out, task_live):
+    ts = amp_tiles.shape[-1]
+    slab, pool = pool_tiles.shape[1], pool_tiles.shape[2]
+    vmem = pl.BlockSpec(memory_space=pltpu.VMEM)
+    hbm = pl.BlockSpec(memory_space=pl.ANY)
+    dma = pltpu.SemaphoreType.DMA
+    out = pl.pallas_call(
+        functools.partial(kernel, n_row, n_col, slab, pool),
+        out_shape=jax.ShapeDtypeStruct((slab * OUT_POOL, ts), jnp.float32),
+        in_specs=[hbm, hbm, vmem, vmem, vmem, vmem],
+        out_specs=vmem,
+        scratch_shapes=[
+            pltpu.VMEM((2 * ts * pool, ts // 2), jnp.float32),
+            pltpu.VMEM((pool, ts, ts), jnp.bfloat16),
+            pltpu.VMEM((pool, ts, ts), jnp.bfloat16),
+            pltpu.VMEM((2 * n_col * n_row * slab, ts // 2), jnp.float32),
+            pltpu.VMEM((pool, slab * OUT_POOL, ts), jnp.bfloat16),
+            pltpu.VMEM((pool, slab * OUT_POOL, ts), jnp.bfloat16),
+            pltpu.VMEM((n_row, 8, 128), jnp.float32),
+            dma((14,)), dma((14,)),
+            dma((n_row,)), dma((n_row,)),
+            dma((n_row,)), dma((n_row,)),
+            dma((4 * (n_col - 1),)), dma((4 * (n_col - 1),)),
+            dma((2,)),
+        ],
+        compiler_params=pltpu.CompilerParams(
+            collective_id=0, has_side_effects=True, vmem_limit_bytes=40 * 2**20),
+    )(
+        by_side(amp_tiles.reshape(ts, ts)), by_side(pool_tiles.reshape(slab * pool, ts)),
+        task_amp[0], task_pool[0], task_out[0], task_live[0],
+    )
+    return out.reshape(1, slab, OUT_POOL, ts)
+
+
 def solution(mesh):
+    n_row, n_col = mesh.shape["row"], mesh.shape["col"]
+
+    def per_device(*arrays):
+        amp_tiles, pool_tiles, task_amp = arrays[0], arrays[1], arrays[2]
+        fits = (
+            n_row == 8 and n_col > 1 and amp_tiles.shape[3] == 256 and amp_tiles.shape[1] == 1
+            and pool_tiles.shape[1] % 16 == 0 and pool_tiles.shape[2] * OUT_POOL == 128
+            and task_amp.shape[-1] <= 128 and 2 * n_col * n_row <= 256
+        )
+        if fits:
+            return slab_plan(n_row, n_col, *arrays)
+        return gathered_plan(*arrays)
+
     in_specs = (
         P("row", "col", None, None),
         P("col", "row", None, None),

time: 173 us -> 43.7 us (0.25)
  waiting for transfers between devices: 98.8 us -> 0 us
  Pallas kernels: 0 us -> 40.1 us
  matrix products: 37.5 us -> 0 us
  local copies, waits for them, and re-layouts: 20.8 us -> 3.39 us
  between operations: 13.1 us -> 0.02 us
  other arithmetic: 2.67 us -> 0 us
    all_gather x2 -> x0, waiting for transfers between devices: 56.7 us -> none  [the longest x1 29.3 us: per_device(): whole_pool = lax.all_gather(pool_tiles, 'row', axis=1, tiled=True)]
    reduce_scatter x1 -> x0, waiting for transfers between devices: 41.4 us -> none  [per_device(): lax.psum_scatter(partial_value, 'row', scatter_dimension=0, tiled=True)]
    pallas_call x0 -> x1, Pallas kernels: none -> 40.1 us  [slab_plan(): pl.pallas_call(functools.partial(kernel, n_row, n_col, slab, pool), out_s...]
    dot_general x2 -> x0, matrix products: 37.5 us -> none  [the longest x1 18.9 us: add_terms(): jnp.einsum('tik,ktj->tij', chosen, integral, precision=lax.Precision.HIGH...]
    gather x2 -> x0, local copies, waits for them, and re-layouts: 18.6 us -> none  [the longest x1 9.75 us: add_terms(): integral = jnp.take(piece[0], pool_index, axis=1)]
  transfers between devices with their start and end apart: 3 -> 0, of which waited for: 3 -> 0; matrix products, arithmetic and copies ran while one was open for 8% -> 0% of each run, Pallas kernels for 0% -> 0%
where the time goes in v1:
time: 43.7 us; the launch traced here: 43.5 us
  Pallas kernels  40.1 us (92%)
  local copies, waits for them, and re-layouts  3.39 us (8%)
    pallas_call x1, Pallas kernels, slab_plan(): pl.pallas_call(functools.partial(kernel, n_row, n_col, slab, pool), out_s...  40.1 us
    unnamed x13, local copies, waits for them, and re-layouts  3.39 us

profile of v1, /device:TPU:0, one launch (start us, length us, event | category | flops | bytes accessed | tf_op | source)
XLA Modules:
  0.0 43.5 jit_solution(12723504420111472170)
XLA Ops:
  0.0 0.0 copy-start.5
  0.0 0.0 copy-start.2
  0.0 0.0 copy-start.3
  0.0 0.0 copy-start.4
  0.0 0.6 %copy-done.5 = s32[1,1,48]{2,1,0:T(1,128)S(1)} copy-done((s32[1,1,48]{2,1,0:T(1,128)S(1)}, s32[1,1,48]{2,1,0:T(1,128)}, u32[]{:S(2)}) %copy-start.5) | copy-done | bytes 216
  0.7 0.0 copy-done.2
  0.7 0.0 copy-done.3
  0.7 0.0 copy-done.4
  0.7 0.0 copy-start
  0.7 1.0 %copy-done = f32[1,32,16,256]{3,2,1,0:T(8,128)S(1)} copy-done((f32[1,32,16,256]{3,2,1,0:T(8,128)S(1)}, f32[1,32,16,256]{3,2,1,0:T(8,128)}, u32[]{:S(2)}) %copy-start) | copy-done | bytes 524312
  1.7 0.0 copy-start.1
  1.7 0.9 %copy-done.1 = f32[1,1,256,256]{3,2,1,0:T(8,128)S(1)} copy-done((f32[1,1,256,256]{3,2,1,0:T(8,128)S(1)}, f32[1,1,256,256]{3,2,1,0:T(8,128)}, u32[]{:S(2)}) %copy-start.1) | copy-done | bytes 262168
  2.7 40.1 %shard_map.64 = f32[256,256]{1,0:T(8,128)S(1)} custom-call(f32[512,128]{1,0:T(8,128)S(1)} %bitcast.17, f32[1024,128]{1,0:T(8,128)S(1)} %bitcast.16, s32[1,48]{1,0:T(1,128)S(1)} %bitcast.18, s32[1,48]{1,0:T(1,128)S(1)} %bitcast.19, s32[1,48]{1,0:T(1,128)S(1)} %bitcast.20, s32[1,48]{1,0:T(1,128)S(1)} %bitcast.21), custom_call_target="tpu_custom_call" | custom-call | tf_op jit(solution)/shard_map/pallas_call | solution.py:275
  42.8 0.7 %copy.8 = f32[1,32,8,256]{3,2,1,0:T(8,128)} copy(f32[1,32,8,256]{3,2,1,0:T(8,128)S(1)} %bitcast.15) | data formatting | bytes 524288
Async XLA Ops:
  0.0 0.7 %copy-start.5 = (s32[1,1,48]{2,1,0:T(1,128)S(1)}, s32[1,1,48]{2,1,0:T(1,128)}, u32[]{:S(2)}) copy-start(s32[1,1,48]{2,1,0:T(1,128)} %param.11) | copy-start | bytes 580
  0.0 0.7 %copy-start.2 = (s32[1,1,48]{2,1,0:T(1,128)S(1)}, s32[1,1,48]{2,1,0:T(1,128)}, u32[]{:S(2)}) copy-start(s32[1,1,48]{2,1,0:T(1,128)} %param.8) | copy-start | bytes 580
  0.0 0.7 %copy-start.3 = (s32[1,1,48]{2,1,0:T(1,128)S(1)}, s32[1,1,48]{2,1,0:T(1,128)}, u32[]{:S(2)}) copy-start(s32[1,1,48]{2,1,0:T(1,128)} %param.9) | copy-start | bytes 580
  0.0 0.7 %copy-start.4 = (s32[1,1,48]{2,1,0:T(1,128)S(1)}, s32[1,1,48]{2,1,0:T(1,128)}, u32[]{:S(2)}) copy-start(s32[1,1,48]{2,1,0:T(1,128)} %param.10) | copy-start | bytes 580
  0.7 1.0 %copy-start = (f32[1,32,16,256]{3,2,1,0:T(8,128)S(1)}, f32[1,32,16,256]{3,2,1,0:T(8,128)}, u32[]{:S(2)}) copy-start(f32[1,32,16,256]{3,2,1,0:T(8,128)} %param.7) | copy-start | bytes 1572868
  1.7 0.9 %copy-start.1 = (f32[1,1,256,256]{3,2,1,0:T(8,128)S(1)}, f32[1,1,256,256]{3,2,1,0:T(8,128)}, u32[]{:S(2)}) copy-start(f32[1,1,256,256]{3,2,1,0:T(8,128)} %param.6) | copy-start | bytes 786436

commit v2 on v1

--- a/solution.py
+++ b/solution.py
@@ -49,11 +49,10 @@
     y_of = r + 4 - 8 * (r // 4)
     d_of = x_of + 4 - 8 * (r // 4)
     vrows = slab * pool * 2
-    half = vrows // 2
+    piece = vrows // 4
     tasks = t_amp.shape[1]
     arows = slab * 2
     blk = n_row * arows
-    chunk = blk // 2
 
     barrier = pltpu.get_barrier_semaphore()
     for d in range(1, n_row):
@@ -83,51 +82,58 @@
     near = (c + n_col - 1) // n_col + (2 * n_col - 2 - c) // n_col
     pl.semaphore_wait(barrier, n_row - 1 + near)
 
+    sib_x = x_of + 1 - 2 * (r % 2)
+    sib_y = y_of + 1 - 2 * (r % 2)
+    sib_d = d_of + 1 - 2 * (r % 2)
+    peers = (sib, sib_x, x_of, sib_y, y_of, sib_d, d_of)
+
     plane = []
-    for d in (6, 2, 4, 3, 5, 7, 1):
-        to = lax.rem(r + d, n_row)
+    for k, to in enumerate(peers):
         copy = pltpu.make_async_remote_copy(
             src_ref=amp_ref.at[pl.ds(pl.multiple_of(to * arows, 8), arows)],
             dst_ref=a_all.at[pl.ds(a_row, arows)],
-            send_sem=p_send.at[d], recv_sem=p_recv.at[d],
+            send_sem=p_send.at[k], recv_sem=p_recv.at[k],
             device_id=(to, c), device_id_type=MESH)
         copy.start()
         plane.append(copy)
 
     def v_copy(index, origin, part, to, own=False):
-        rows = pl.ds(pl.multiple_of(origin * vrows + part * half, 8), half)
-        src = pool_ref.at[pl.ds(part * half, half)] if own else v_all.at[rows]
+        rows = pl.ds(pl.multiple_of(origin * vrows + part * piece, 8), piece)
+        src = pool_ref.at[pl.ds(part * piece, piece)] if own else v_all.at[rows]
         return pltpu.make_async_remote_copy(
             src_ref=src, dst_ref=v_all.at[rows],
             send_sem=v_send.at[index], recv_sem=v_recv.at[index],
             device_id=(to, c), device_id_type=MESH)
 
-    v = [
-        v_copy(0, r, 0, x_of, True), v_copy(1, r, 1, x_of, True),
-        v_copy(2, r, 1, y_of, True), v_copy(3, r, 0, y_of, True),
-        v_copy(4, r, 0, sib, True), v_copy(5, r, 1, sib, True),
-        v_copy(6, x_of, 0, y_of), v_copy(7, x_of, 0, sib),
-        v_copy(8, y_of, 1, x_of), v_copy(9, y_of, 1, sib),
-        v_copy(10, x_of, 1, sib), v_copy(11, y_of, 0, sib),
-        v_copy(12, d_of, 0, sib), v_copy(13, d_of, 1, sib),
-    ]
-    for index in (0, 2, 1, 3, 4, 5):
-        v[index].start()
+    to_x = [v_copy(q, r, q, x_of, True) for q in range(4)]
+    to_y = [v_copy(4 + q, r, q, y_of, True) for q in range(4)]
+    to_s = [v_copy(8 + q, r, q, sib, True) for q in range(4)]
+    far = [v_copy(12 + q, x_of, q, y_of) if q < 2 else v_copy(12 + q, y_of, q, x_of) for q in range(4)]
+    x_s = [v_copy(16 + q, x_of, q, sib) for q in range(4)]
+    y_s = [v_copy(20 + q, y_of, q, sib) for q in range(4)]
+    d_s = [v_copy(24 + q, d_of, q, sib) for q in range(4)]
+    for q in range(4):
+        to_x[q].start()
+        to_y[3 - q].start()
+    for q in range(4):
+        to_s[q].start()
 
     lists = []
-    for d in range(1, n_row):
+    for k, to in enumerate(peers):
         copy = pltpu.make_async_remote_copy(
             src_ref=info.at[r], dst_ref=info.at[r],
-            send_sem=i_send.at[d], recv_sem=i_recv.at[d],
-            device_id=(lax.rem(r + d, n_row), c), device_id_type=MESH)
+            send_sem=i_send.at[k], recv_sem=i_recv.at[k],
+            device_id=(to, c), device_id_type=MESH)
         copy.start()
         lists.append(copy)
+
+    bases = [one - one % 2 for one in (r, x_of, y_of, d_of)]
 
     def z_copy(way, step, part):
         tile = c - step if way == 0 else c + step
         to = c + 1 if way == 0 else c - 1
-        rows = pl.ds(pl.multiple_of(tile * blk + part * chunk, 8), chunk)
-        slot = ((way * (n_col - 1)) + step) * 2 + part
+        rows = pl.ds(pl.multiple_of(tile * blk + bases[part] * arows, 8), 2 * arows)
+        slot = ((way * (n_col - 1)) + step) * 4 + part
         return pltpu.make_async_remote_copy(
             src_ref=a_all.at[rows], dst_ref=a_all.at[rows],
             send_sem=z_send.at[slot], recv_sem=z_recv.at[slot],
@@ -154,6 +160,21 @@
                 z_copy(way, step, part).wait_recv()
         if step + 1 < n_col - 1:
             z_start(step + 1, part)
+
+    def near_land(q):
+        to_x[q].wait_recv()
+        if q < 2:
+            far[q].start()
+        x_s[q].start()
+        to_y[3 - q].wait_recv()
+        if q < 2:
+            far[3 - q].start()
+        y_s[3 - q].start()
+
+    def far_land(q):
+        for one in (q, 3 - q):
+            far[one].wait_recv()
+            d_s[one].start()
 
     def split_pool(origin):
         def one(p, carry):
@@ -167,12 +188,43 @@
         lax.fori_loop(0, pool, one, 0, unroll=4)
 
     own_a.wait()
-    for copy in plane:
-        copy.wait_recv()
+    plane[0].wait_recv()
     z_start(0, 0)
-    z_start(0, 1)
+    for part in range(1, 4):
+        plane[2 * part - 1].wait_recv()
+        plane[2 * part].wait_recv()
+        z_start(0, part)
     own_v.wait()
     split_pool(r)
+
+    z_events = [(step, part) for step in range(n_col - 1) for part in range(4)]
+    v_events = [(near_land, 0), (near_land, 1), (near_land, 2), (near_land, 3), (far_land, 0), (far_land, 1)]
+    order = z_events[:2]
+    rest = z_events[2:]
+    for at, event in enumerate(v_events):
+        share = len(rest) * (at + 1) // (len(v_events) + 1)
+        done = len(rest) * at // (len(v_events) + 1)
+        order = order + rest[done:share] + [event]
+    order = order + rest[len(rest) * len(v_events) // (len(v_events) + 1):]
+    for first, second in order:
+        if callable(first):
+            first(second)
+            if (first, second) == v_events[1]:
+                for copy in to_s:
+                    copy.wait_recv()
+                split_pool(sib)
+            if (first, second) == v_events[3]:
+                split_pool(x_of)
+                split_pool(y_of)
+            if (first, second) == v_events[4]:
+                for copy in x_s + y_s:
+                    copy.wait_recv()
+                split_pool(sib_x)
+                split_pool(sib_y)
+        else:
+            z_land(first, second)
+    split_pool(d_of)
+
     for copy in lists:
         copy.wait_recv()
     entry = lax.broadcasted_iota(jnp.int32, (pool * OUT_POOL, 128), 0).astype(jnp.float32)
@@ -188,36 +240,6 @@
         jnp.concatenate(starts, axis=1).astype(jnp.bfloat16),
         (((1,), (1,)), ((), ())), preferred_element_type=jnp.float32).astype(jnp.bfloat16)
 
-    z_land(0, 0)
-    v[0].wait_recv()
-    v[6].start()
-    v[7].start()
-    v[2].wait_recv()
-    v[8].start()
-    v[9].start()
-    z_land(0, 1)
-    for index in (4, 5):
-        v[index].wait_recv()
-    split_pool(sib)
-    if n_col > 2:
-        z_land(1, 0)
-        z_land(1, 1)
-    v[1].wait_recv()
-    v[10].start()
-    v[3].wait_recv()
-    v[11].start()
-    split_pool(x_of)
-    split_pool(y_of)
-    for step in range(2, n_col - 1):
-        z_land(step, 0)
-    v[6].wait_recv()
-    v[12].start()
-    v[8].wait_recv()
-    v[13].start()
-    split_pool(d_of)
-    for step in range(2, n_col - 1):
-        z_land(step, 1)
-
     def spread(pair, carry):
         parts = []
         for k in range(2):
@@ -232,15 +254,10 @@
         m_hi[:, at, :] = high
         m_lo[:, at, :] = low
         return carry
-    lax.fori_loop(0, slab // 2, spread, 0, unroll=2)
-
-    for index in (7, 9, 10, 11, 12, 13):
-        v[index].wait_recv()
-    sib_x = x_of + 1 - 2 * (r % 2)
-    sib_y = y_of + 1 - 2 * (r % 2)
-    sib_d = d_of + 1 - 2 * (r % 2)
-    split_pool(sib_x)
-    split_pool(sib_y)
+    lax.fori_loop(0, slab // 2, spread, 0, unroll=4)
+
+    for copy in d_s:
+        copy.wait_recv()
     split_pool(sib_d)
 
     total = jnp.zeros(out_ref.shape, jnp.float32)
@@ -250,13 +267,13 @@
         total = total + jnp.dot(m_lo[p], v_hi[p], preferred_element_type=jnp.float32)
     out_ref[...] = total
 
-    for copy in plane + lists + v:
+    for copy in plane + lists + to_x + to_y + to_s + far + x_s + y_s + d_s:
         copy.wait_send()
     for step in range(n_col - 1):
         for way in range(2):
             @pl.when(z_sends(way, step))
             def _():
-                for part in range(2):
+                for part in range(4):
                     z_copy(way, step, part).wait_send()
 
 
@@ -285,14 +302,14 @@
             pltpu.VMEM((pool, slab * OUT_POOL, ts), jnp.bfloat16),
             pltpu.VMEM((pool, slab * OUT_POOL, ts), jnp.bfloat16),
             pltpu.VMEM((n_row, 8, 128), jnp.float32),
-            dma((14,)), dma((14,)),
+            dma((28,)), dma((28,)),
             dma((n_row,)), dma((n_row,)),
             dma((n_row,)), dma((n_row,)),
-            dma((4 * (n_col - 1),)), dma((4 * (n_col - 1),)),
+            dma((8 * (n_col - 1),)), dma((8 * (n_col - 1),)),
             dma((2,)),
         ],
         compiler_params=pltpu.CompilerParams(
-            collective_id=0, has_side_effects=True, vmem_limit_bytes=40 * 2**20),
+            collective_id=0, has_side_effects=True, vmem_limit_bytes=60 * 2**20),
     )(
         by_side(amp_tiles.reshape(ts, ts)), by_side(pool_tiles.reshape(slab * pool, ts)),
         task_amp[0], task_pool[0], task_out[0], task_live[0],

time: 43.7 us -> 34.5 us (0.79)
  Pallas kernels: 40.1 us -> 32.6 us
  local copies, waits for them, and re-layouts: 3.39 us -> 1.67 us
    pallas_call x1, Pallas kernels: 40.1 us -> 32.6 us  [slab_plan(): pl.pallas_call(functools.partial(kernel, n_row, n_col, slab, pool), out_s...]
    unnamed x13 -> x1, local copies, waits for them, and re-layouts: 3.39 us -> 1.67 us
where the time goes in v2:
time: 34.5 us; the launch traced here: 34.3 us
  Pallas kernels  32.6 us (94%)
  local copies, waits for them, and re-layouts  1.67 us (5%)
    pallas_call x1, Pallas kernels, slab_plan(): pl.pallas_call(functools.partial(kernel, n_row, n_col, slab, pool), out_s...  32.6 us
    unnamed x1, local copies, waits for them, and re-layouts  1.67 us

profile of v2, /device:TPU:0, one launch (start us, length us, event | category | flops | bytes accessed | tf_op | source)
XLA Modules:
  0.0 34.3 jit_solution(9222793936581640465)
XLA Ops:
  0.0 32.6 %shard_map.64 = f32[256,256]{1,0:T(8,128)} custom-call(f32[512,128]{1,0:T(8,128)} %bitcast.17, f32[1024,128]{1,0:T(8,128)} %bitcast.16, s32[1,48]{1,0:T(1,128)} %bitcast.18, s32[1,48]{1,0:T(1,128)} %bitcast.19, s32[1,48]{1,0:T(1,128)} %bitcast.20, s32[1,48]{1,0:T(1,128)} %bitcast.21), custom_call_target="tpu_custom_call" | custom-call | tf_op jit(solution)/shard_map/pallas_call | solution.py:292
  32.6 1.7 %copy.8 = f32[1,32,8,256]{3,2,1,0:T(8,128)} copy(f32[1,32,8,256]{3,2,1,0:T(8,128)} %bitcast.15) | data formatting | bytes 524288

commit v3 on v2

--- a/solution.py
+++ b/solution.py
@@ -97,6 +97,15 @@
         copy.start()
         plane.append(copy)
 
+    lists = []
+    for k, to in enumerate(peers):
+        copy = pltpu.make_async_remote_copy(
+            src_ref=info.at[r], dst_ref=info.at[r],
+            send_sem=i_send.at[k], recv_sem=i_recv.at[k],
+            device_id=(to, c), device_id_type=MESH)
+        copy.start()
+        lists.append(copy)
+
     def v_copy(index, origin, part, to, own=False):
         rows = pl.ds(pl.multiple_of(origin * vrows + part * piece, 8), piece)
         src = pool_ref.at[pl.ds(part * piece, piece)] if own else v_all.at[rows]
@@ -118,15 +127,6 @@
     for q in range(4):
         to_s[q].start()
 
-    lists = []
-    for k, to in enumerate(peers):
-        copy = pltpu.make_async_remote_copy(
-            src_ref=info.at[r], dst_ref=info.at[r],
-            send_sem=i_send.at[k], recv_sem=i_recv.at[k],
-            device_id=(to, c), device_id_type=MESH)
-        copy.start()
-        lists.append(copy)
-
     bases = [one - one % 2 for one in (r, x_of, y_of, d_of)]
 
     def z_copy(way, step, part):
@@ -186,6 +186,22 @@
             v_lo[p, at, :] = low
             return carry
         lax.fori_loop(0, pool, one, 0, unroll=4)
+
+    def count_tasks():
+        for copy in lists:
+            copy.wait_recv()
+        entry = lax.broadcasted_iota(jnp.int32, (pool * OUT_POOL, 128), 0).astype(jnp.float32)
+        line = lax.broadcasted_iota(jnp.int32, (2 * n_col * n_row, 128), 0)
+        line_row = line % n_row
+        line_amp = ((line // n_row) % n_col).astype(jnp.float32)
+        ends, starts = [], []
+        for other in range(n_row):
+            ends.append(jnp.where(entry == info[other, 1:2, :], 1.0, 0.0))
+            starts.append(jnp.where(jnp.logical_and(line_row == other, line_amp == info[other, 0:1, :]), 1.0, 0.0))
+        return lax.dot_general(
+            jnp.concatenate(ends, axis=1).astype(jnp.bfloat16),
+            jnp.concatenate(starts, axis=1).astype(jnp.bfloat16),
+            (((1,), (1,)), ((), ())), preferred_element_type=jnp.float32).astype(jnp.bfloat16)
 
     own_a.wait()
     plane[0].wait_recv()
@@ -213,6 +229,8 @@
                 for copy in to_s:
                     copy.wait_recv()
                 split_pool(sib)
+            if (first, second) == v_events[2]:
+                count = count_tasks()
             if (first, second) == v_events[3]:
                 split_pool(x_of)
                 split_pool(y_of)
@@ -224,21 +242,6 @@
         else:
             z_land(first, second)
     split_pool(d_of)
-
-    for copy in lists:
-        copy.wait_recv()
-    entry = lax.broadcasted_iota(jnp.int32, (pool * OUT_POOL, 128), 0).astype(jnp.float32)
-    line = lax.broadcasted_iota(jnp.int32, (2 * n_col * n_row, 128), 0)
-    line_row = line % n_row
-    line_amp = ((line // n_row) % n_col).astype(jnp.float32)
-    ends, starts = [], []
-    for other in range(n_row):
-        ends.append(jnp.where(entry == info[other, 1:2, :], 1.0, 0.0))
-        starts.append(jnp.where(jnp.logical_and(line_row == other, line_amp == info[other, 0:1, :]), 1.0, 0.0))
-    count = lax.dot_general(
-        jnp.concatenate(ends, axis=1).astype(jnp.bfloat16),
-        jnp.concatenate(starts, axis=1).astype(jnp.bfloat16),
-        (((1,), (1,)), ((), ())), preferred_element_type=jnp.float32).astype(jnp.bfloat16)
 
     def spread(pair, carry):
         parts = []
@@ -254,7 +257,7 @@
         m_hi[:, at, :] = high
         m_lo[:, at, :] = low
         return carry
-    lax.fori_loop(0, slab // 2, spread, 0, unroll=4)
+    lax.fori_loop(0, slab // 2, spread, 0, unroll=8)
 
     for copy in d_s:
         copy.wait_recv()

time: 34.5 us -> 34.1 us (0.988)
  Pallas kernels: 32.6 us -> 32.2 us
    pallas_call x1, Pallas kernels: 32.6 us -> 32.2 us  [slab_plan(): pl.pallas_call(functools.partial(kernel, n_row, n_col, slab, pool), out_s...]
where the time goes in v3:
time: 34.1 us; the launch traced here: 33.9 us
  Pallas kernels  32.2 us (94%)
  local copies, waits for them, and re-layouts  1.67 us (5%)
    pallas_call x1, Pallas kernels, slab_plan(): pl.pallas_call(functools.partial(kernel, n_row, n_col, slab, pool), out_s...  32.2 us
    unnamed x1, local copies, waits for them, and re-layouts  1.67 us

profile of v3, /device:TPU:0, one launch (start us, length us, event | category | flops | bytes accessed | tf_op | source)
XLA Modules:
  0.0 33.9 jit_solution(8490136849698971676)
XLA Ops:
  0.0 32.2 %shard_map.64 = f32[256,256]{1,0:T(8,128)} custom-call(f32[512,128]{1,0:T(8,128)} %bitcast.17, f32[1024,128]{1,0:T(8,128)} %bitcast.16, s32[1,48]{1,0:T(1,128)} %bitcast.18, s32[1,48]{1,0:T(1,128)} %bitcast.19, s32[1,48]{1,0:T(1,128)} %bitcast.20, s32[1,48]{1,0:T(1,128)} %bitcast.21), custom_call_target="tpu_custom_call" | custom-call | tf_op jit(solution)/shard_map/pallas_call | solution.py:295
  32.3 1.7 %copy.8 = f32[1,32,8,256]{3,2,1,0:T(8,128)} copy(f32[1,32,8,256]{3,2,1,0:T(8,128)} %bitcast.15) | data formatting | bytes 524288
